TPU v7x, 32 devices: a whole 2x2x4 slice. The times are simulated.
32 devices in a mesh: clips: 2 (over y), pix: 4 (over z), pair: 2 (over x), dir: 2 (over core).
Axes of the slice: x: 2, y: 2, z: 4, core: 2. Of those that a mesh axis runs over, the one named last changes fastest.
Arguments:
- features: bfloat16 [4, 2, 1920, 128], P(('clips', 'pair'), 'dir', 'pix'), parts along dimension 0, may hold values from -6 to 6
Outputs:
- flow: float32 [4, 2, 2, 1920], P(('clips', 'pair'), 'dir', None, 'pix'), parts along dimension 0
- matched: bfloat16 [4, 2, 1920, 128], P(('clips', 'pair'), 'dir', 'pix'), parts along dimension 0
There are 2 independent parts, one for each index of `clips`. A program takes and returns all parts, laid end to end along the dimension named above; each array names one. Nothing has to cross between parts.
All inputs are finite; a program needn't handle non-finite values.
Results may differ from a plain program's by a relative error of at most 0.0065.
Values may be sent and summed in bfloat16 or wider, within the bound.
A program may use at most 64 MiB of HBM per device.

v0:
```python
import jax
import jax.numpy as jnp
from jax import lax
from jax.sharding import PartitionSpec as P

C = 128
W = 120


def from_partner(array, axis, bit):
    return lax.ppermute(array, axis, [(i, i ^ 1 << bit) for i in range(lax.axis_size(axis))])


def positions(index):
    return ((index % W).astype(jnp.float32) / W, (index // W).astype(jnp.float32) / W)


def fold_part(carry, queries, keys, start):
    top, total, sum_x, sum_y, acc = carry
    scores = lax.dot_general(
        queries, keys, (((1,), (1,)), ((), ())), preferred_element_type=jnp.float32
    ) * C ** (-0.5)
    posx, posy = positions(start + jnp.arange(keys.shape[0], dtype=jnp.int32))
    new_top = jnp.maximum(top, jnp.max(scores, axis=1))
    fade = jnp.exp(top - new_top)
    weights = jnp.exp(scores - new_top[:, None])
    total = total * fade + jnp.sum(weights, axis=1)
    sum_x = sum_x * fade + jnp.sum(weights * posx[None, :], axis=1)
    sum_y = sum_y * fade + jnp.sum(weights * posy[None, :], axis=1)
    acc = acc * fade[:, None] + jnp.dot(
        weights.astype(jnp.bfloat16), keys, preferred_element_type=jnp.float32
    )
    return (new_top, total, sum_x, sum_y, acc)


def make_step(queries, carry, piece):
    keys = piece.reshape(-1, piece.shape[-1])
    length = keys.shape[0]
    width = length
    while width > 1536 and width % 2 == 0:
        width = width // 2
    blocks = keys.reshape(length // width, width, keys.shape[1])

    def inner(state, item):
        return (fold_part(state, queries, item[0], item[1] * width), None)

    result, unused = lax.scan(inner, carry, (blocks, jnp.arange(length // width, dtype=jnp.int32)))
    return result


def finish(carry, first_row):
    top, total, sum_x, sum_y, acc = carry
    own_x, own_y = positions(first_row + jnp.arange(total.shape[0], dtype=jnp.int32))
    flow = jnp.stack([sum_x / total - own_x, sum_y / total - own_y])
    matched = (acc / total[:, None]).astype(jnp.bfloat16)
    return (flow, matched)


def body(features):
    rows_here = features.shape[2]
    chans = features.shape[3]
    first_row = lax.axis_index("pix") * rows_here
    init = (
        jnp.full((rows_here,), -jnp.inf, jnp.float32),
        jnp.zeros((rows_here,), jnp.float32),
        jnp.zeros((rows_here,), jnp.float32),
        jnp.zeros((rows_here,), jnp.float32),
        jnp.zeros((rows_here, chans), jnp.float32),
    )
    foreign = from_partner(features, "dir", 0)
    carry = make_step(
        foreign.reshape(rows_here, chans), init, lax.all_gather(features, "pix", axis=2, tiled=True)
    )
    other_flow, other_matched = finish(carry, first_row)
    flow, wide_matched = (
        from_partner(other_flow.astype(jnp.bfloat16), "dir", 0).astype(other_flow.dtype),
        from_partner(other_matched.astype(jnp.float32).astype(jnp.bfloat16), "dir", 0).astype(
            jnp.float32
        ),
    )
    matched = wide_matched.astype(jnp.bfloat16)
    return (flow.reshape(1, 1, 2, rows_here), matched.reshape(1, 1, rows_here, chans))


def solution(mesh):
    placed = (P(("clips", "pair"), "dir", "pix", None),)
    return jax.shard_map(
        body,
        mesh=mesh,
        in_specs=placed,
        out_specs=(
            P(("clips", "pair"), "dir", None, "pix"),
            P(("clips", "pair"), "dir", "pix", None),
        ),
        check_vma=False,
    )
```

profile of v0, /device:TPU:0, one launch (start us, length us, event | category | flops | bytes accessed | tf_op | source)
XLA Modules:
  0.0 27.1 jit_solution(562660175791292851)
XLA Ops:
  0.6 0.5 %collective-permute-start = (bf16[1,1,480,128]{3,2,1,0:T(8,128)(2,1)}, bf16[1,1,480,128]{3,2,1,0:T(8,128)(2,1)S(1)}, u32[]{:S(2)}, u32[]{:S(2)}) collective-permute-start(bf16[1,1,480,128]{3,2,1,0:T(8,128)(2,1)} %param.3), channel_id=1, source_target_pairs={{0,1},{1,0},{2,3},{3,2},{4,5},{5,4},{6,7},{7,6},{8,9},{9,8},{10,11... | collective-permute-start | bytes 368648 | tf_op jit(solution)/shard_map/ppermute | solution.py:11
  1.2 17.3 %all_gather.3 = bf16[1,1,1920,128]{3,2,1,0:T(8,128)(2,1)S(1)} all-gather(bf16[1,1,480,128]{3,2,1,0:T(8,128)(2,1)} %param.3), channel_id=1, replica_groups=mesh['clips'=2,'pix'=4,'pair'=2,'dir'=2] {'pix'}, dimensions={2}, use_global_device_ids=true | all-gather | bytes 614400 | tf_op jit(solution)/shard_map/all_gather | solution.py:72
  18.5 0.0 collective-permute-done
  18.5 6.0 %while.21 = (s32[]{:T(128)}, f32[480]{0:T(512)S(1)}, f32[480]{0:T(512)S(1)}, f32[480]{0:T(512)S(1)}, f32[480]{0:T(512)S(1)}, /*index=5*/f32[480,128]{1,0:T(8,128...) while((s32[]{:T(128)}, f32[480]{0:T(512)S(1)}, ...), condition=%wide.region_5.6_spmd.clone, body=%wide.region_0.5_spmd.clone.sunk | while | flops 241664160 | bytes 6822190 | solution.py:47
  18.5 0.6 %dynamic_slice.31 = s32[1]{0:T(128)} dynamic-slice(s32[2]{0:T(128)S(1)} %get-tuple-element.295, s32[]{:T(128)S(6)} %copy.9), dynamic_slice_sizes={1} | dynamic-slice | bytes 12 | tf_op jit(solution)/shard_map/while/body/jit(dynamic_index_in_dim)/dynamic_slice | solution.py:47
  19.8 0.5 %multiply_reduce_fusion.5 = (f32[480]{0:T(512)S(1)}, f32[960,480]{1,0:T(8,128)S(1)}) fusion(bf16[480,128]{1,0:T(8,128)(2,1)S(1)} %get-tuple-element.294, bf16[2,960,128]{2,1,0:T(8,128)(2,1)S(1)} %get-tuple-element.293, s32[]{:T(128)S(6)} %copy.9), kind=kOutput, calls=%fused_computation.3.clone.1 | convolution fusion | flops 118885920 | bytes 2213764 | tf_op jit(solution)/shard_map/while/body/eval_jaxpr/dot_general | solution.py:20
  20.3 0.6 %multiply_reduce_fusion.6 = (f32[480]{0:T(512)S(1)}, f32[480]{0:T(512)S(1)}, f32[480]{0:T(512)S(1)}) fusion(f32[960]{0:T(1024)S(1)} %get-tuple-element.253, f32[480]{0:T(512)S(1)} %select_maximum_fusion.2, f32[960,480]{1,0:T(8,128)S(1)} %get-tuple-element.254, f32[960]{0:T(1024)S(1)} %get-tuple-element.255), kind=kLoop, calls=%fused_computation.clone.1 | loop fusion | flops 3224160 | bytes 1858560 | tf_op jit(solution)/shard_map/while/body/eval_jaxpr/reduce_sum | solution.py:29
  21.0 0.5 %convolution_add_fusion.2 = f32[480,128]{1,0:T(8,128)S(1)} fusion(f32[960,480]{1,0:T(8,128)S(1)} %get-tuple-element.254, f32[480]{0:T(512)S(1)} %select_maximum_fusion.2, f32[480,128]{1,0:T(8,128)S(1)} %get-tuple-element.280, bf16[2,960,128]{2,1,0:T(8,128)(2,1)S(1)} %get-tuple-element.293, s32[]{:T(128)S(6)} %copy.9, f32[480]{0:T(512)S(1)} %get-tuple-element.258, ...), kind=kOutput, calls=%fused_computation.4.clone.1 | convolution fusion | flops 119531520 | bytes 2707461 | tf_op jit(solution)/shard_map/while/body/eval_jaxpr/dot_general | solution.py:30
  21.5 0.6 %dynamic_slice.31 = s32[1]{0:T(128)} dynamic-slice(s32[2]{0:T(128)S(1)} %get-tuple-element.295, s32[]{:T(128)S(6)} %copy.9), dynamic_slice_sizes={1} | dynamic-slice | bytes 12 | tf_op jit(solution)/shard_map/while/body/jit(dynamic_index_in_dim)/dynamic_slice | solution.py:47
  22.8 0.5 %multiply_reduce_fusion.5 = (f32[480]{0:T(512)S(1)}, f32[960,480]{1,0:T(8,128)S(1)}) fusion(bf16[480,128]{1,0:T(8,128)(2,1)S(1)} %get-tuple-element.294, bf16[2,960,128]{2,1,0:T(8,128)(2,1)S(1)} %get-tuple-element.293, s32[]{:T(128)S(6)} %copy.9), kind=kOutput, calls=%fused_computation.3.clone.1 | convolution fusion | flops 118885920 | bytes 2213764 | tf_op jit(solution)/shard_map/while/body/eval_jaxpr/dot_general | solution.py:20
  23.3 0.6 %multiply_reduce_fusion.6 = (f32[480]{0:T(512)S(1)}, f32[480]{0:T(512)S(1)}, f32[480]{0:T(512)S(1)}) fusion(f32[960]{0:T(1024)S(1)} %get-tuple-element.253, f32[480]{0:T(512)S(1)} %select_maximum_fusion.2, f32[960,480]{1,0:T(8,128)S(1)} %get-tuple-element.254, f32[960]{0:T(1024)S(1)} %get-tuple-element.255), kind=kLoop, calls=%fused_computation.clone.1 | loop fusion | flops 3224160 | bytes 1858560 | tf_op jit(solution)/shard_map/while/body/eval_jaxpr/reduce_sum | solution.py:29
  24.0 0.5 %convolution_add_fusion.2 = f32[480,128]{1,0:T(8,128)S(1)} fusion(f32[960,480]{1,0:T(8,128)S(1)} %get-tuple-element.254, f32[480]{0:T(512)S(1)} %select_maximum_fusion.2, f32[480,128]{1,0:T(8,128)S(1)} %get-tuple-element.280, bf16[2,960,128]{2,1,0:T(8,128)(2,1)S(1)} %get-tuple-element.293, s32[]{:T(128)S(6)} %copy.9, f32[480]{0:T(512)S(1)} %get-tuple-element.258, ...), kind=kOutput, calls=%fused_computation.4.clone.1 | convolution fusion | flops 119531520 | bytes 2707461 | tf_op jit(solution)/shard_map/while/body/eval_jaxpr/dot_general | solution.py:30
  24.6 0.1 collective-permute-start.1
  24.7 0.1 divide_convert_fusion
  24.8 0.6 %collective-permute-start.2 = (bf16[480,128]{1,0:T(8,128)(2,1)S(1)}, bf16[480,128]{1,0:T(8,128)(2,1)S(1)}, u32[]{:S(2)}, u32[]{:S(2)}) collective-permute-start(bf16[480,128]{1,0:T(8,128)(2,1)S(1)} %divide_convert_fusion), channel_id=1, source_target_pairs={{0,1},{1,0},{2,3},{3,2},{4,5},{5,4},{6,7},{7,6},{8,9},{9,8},{10,11... | collective-permute-start | bytes 368648 | tf_op jit(solution)/shard_map/ppermute | solution.py:11
  25.4 0.4 %collective-permute-done.1 = bf16[2,480]{1,0:T(2,128)(2,1)S(1)} collective-permute-done((bf16[2,480]{1,0:T(2,128)(2,1)S(1)}, bf16[2,480]{1,0:T(2,128)(2,1)S(1)}, u32[]{:S(2)}, u32[]{:S(2)}) %collective-permute-start.1) | collective-permute-done | bytes 1952 | tf_op jit(solution)/shard_map/ppermute | solution.py:11
  25.8 0.6 %bitcast_convert_fusion = f32[1,1,2,480]{3,2,1,0:T(2,128)} fusion(bf16[2,480]{1,0:T(2,128)(2,1)S(1)} %collective-permute-done.1), kind=kLoop, calls=%fused_computation.45 | loop fusion | flops 960 | bytes 5760 | tf_op jit(solution)/shard_map/reshape | solution.py:82
  26.4 0.0 collective-permute-done.2
  26.4 0.6 %copy.22 = bf16[1,1,480,128]{3,2,1,0:T(8,128)(2,1)} copy(bf16[1,1,480,128]{3,2,1,0:T(8,128)(2,1)S(1)} %bitcast.25) | data formatting | bytes 245760
  (20 shorter events, 0.2 us)
Async XLA Ops:
  0.6 17.9 %collective-permute-start = (bf16[1,1,480,128]{3,2,1,0:T(8,128)(2,1)}, bf16[1,1,480,128]{3,2,1,0:T(8,128)(2,1)S(1)}, u32[]{:S(2)}, u32[]{:S(2)}) collective-permute-start(bf16[1,1,480,128]{3,2,1,0:T(8,128)(2,1)} %param.3), channel_id=1, source_target_pairs={{0,1},{1,0},{2,3},{3,2},{4,5},{5,4},{6,7},{7,6},{8,9},{9,8},{10,11... | collective-permute-start | bytes 368648 | tf_op jit(solution)/shard_map/ppermute | solution.py:11
  24.6 1.2 %collective-permute-start.1 = (bf16[2,480]{1,0:T(2,128)(2,1)S(1)}, bf16[2,480]{1,0:T(2,128)(2,1)S(1)}, u32[]{:S(2)}, u32[]{:S(2)}) collective-permute-start(bf16[2,480]{1,0:T(2,128)(2,1)S(1)} %pad_maximum_fusion), channel_id=1, source_target_pairs={{0,1},{1,0},{2,3},{3,2},{4,5},{5,4},{6,7},{7,6},{8,9},{9,8},{10,11... | collective-permute-start | bytes 5768 | tf_op jit(solution)/shard_map/ppermute | solution.py:11
  24.8 1.6 %collective-permute-start.2 = (bf16[480,128]{1,0:T(8,128)(2,1)S(1)}, bf16[480,128]{1,0:T(8,128)(2,1)S(1)}, u32[]{:S(2)}, u32[]{:S(2)}) collective-permute-start(bf16[480,128]{1,0:T(8,128)(2,1)S(1)} %divide_convert_fusion), channel_id=1, source_target_pairs={{0,1},{1,0},{2,3},{3,2},{4,5},{5,4},{6,7},{7,6},{8,9},{9,8},{10,11... | collective-permute-start | bytes 368648 | tf_op jit(solution)/shard_map/ppermute | solution.py:11
where the time goes:
time: 27.3 us; the launch traced here: 27.1 us
  blocking collectives  17.3 us (63%)
  other arithmetic  2.18 us (8%)
  matrix products  2.06 us (8%)
  local copies, waits for them, and re-layouts  1.84 us (7%)
  loops' own time  1.38 us (5%)
  starting transfers between devices  1.15 us (4%)
  between operations  0.68 us (2%)
  waiting for transfers between devices  0.44 us (2%)
    all_gather x1, blocking collectives, body(): lax.all_gather(features, 'pix', axis=2, tiled=True)  17.3 us
    another operation x1, loops' own time, make_step(): lax.scan(inner, carry, (blocks, jnp.arange(length // width, dtype=jnp.int...  1.38 us
    reduce_sum x2, other arithmetic, fold_part(): sum_y = sum_y * fade + jnp.sum(weights * posy[None, :], axis=1)  1.29 us
    dynamic_slice x2, local copies, waits for them, and re-layouts, make_step(): lax.scan(inner, carry, (blocks, jnp.arange(length // width, dtype=jnp.int...  1.17 us
    ppermute x3, starting transfers between devices, from_partner(): lax.ppermute(array, axis, [(i, i ^ 1 << bit) for i in range(lax.axis_size...  1.15 us
    dot_general x2, matrix products, fold_part(): jnp.dot(weights.astype(jnp.bfloat16), keys, preferred_element_type=jnp.fl...  1.06 us
    dot_general x2, matrix products, fold_part(): lax.dot_general(queries, keys, (((1,), (1,)), ((), ())), preferred_elemen...  0.99 us
    unnamed x1, local copies, waits for them, and re-layouts  0.65 us
  transfers between devices with their start and end apart: 3, of which 1 were waited for; matrix products, arithmetic and copies ran while one was open for 3% of the time, Pallas kernels for 0%

commit v1 on v0

v1 whole, which is shorter than its diff:
```python
import functools
import math

import jax
import jax.numpy as jnp
from jax import lax
from jax.experimental import pallas as pl
from jax.experimental.pallas import tpu as pltpu
from jax.sharding import PartitionSpec as P

W = 120
LOWEST = -1e30
PARTS = 2
WIDTH = 512
SUMS = 16
LIMIT = 40 * 2**20
MESH = pl.DeviceIdType.MESH


def grid_position(index):
    row = jnp.floor((index + 0.5) * (1.0 / W))
    return index - row * W, row


def kernel(
    count, feats, flow, matched, queries, held, places, top, acc, own_sem, pass_sem, recv_sem, load_sem
):
    rows, chans = feats.shape[2], feats.shape[3]
    part = rows // PARTS
    scale = math.log2(math.e) / math.sqrt(chans)
    here = lax.axis_index("pix")
    side = lax.axis_index("dir")
    other = 1 - side
    has_left = here > 0
    has_right = here < count - 1

    load = pltpu.make_async_copy(feats.at[0, 0], queries, load_sem)
    load.start()

    barrier = pltpu.get_barrier_semaphore()

    def greet(pix, core):
        pl.semaphore_signal(
            barrier, inc=1, device_id={"pix": pix, "dir": core}, device_id_type=MESH
        )

    greet(here, other)

    @pl.when(has_left)
    def _():
        greet(here - 1, other)
        greet(here - 1, side)

    @pl.when(has_right)
    def _():
        greet(here + 1, other)
        greet(here + 1, side)

    neighbours = has_left.astype(jnp.int32) + has_right.astype(jnp.int32)
    pl.semaphore_wait(barrier, 1 + 2 * neighbours)

    def own_copy(which, pix, piece):
        span = pl.ds(piece * part, part)
        return pltpu.make_async_remote_copy(
            src_ref=feats.at[0, 0, span],
            dst_ref=held.at[here, span],
            send_sem=own_sem.at[which, piece],
            recv_sem=recv_sem.at[here, piece],
            device_id={"pix": pix, "dir": other},
            device_id_type=MESH,
        )

    def pass_copy(slot, pix, piece):
        span = pl.ds(piece * part, part)
        return pltpu.make_async_remote_copy(
            src_ref=held.at[slot, span],
            dst_ref=held.at[slot, span],
            send_sem=pass_sem.at[slot, piece],
            recv_sem=recv_sem.at[slot, piece],
            device_id={"pix": pix, "dir": side},
            device_id_type=MESH,
        )

    for piece in range(PARTS):

        @pl.when(has_left)
        def _():
            own_copy(1, here - 1, piece).start()

        @pl.when(has_right)
        def _():
            own_copy(2, here + 1, piece).start()

    for piece in range(PARTS):
        own_copy(0, here, piece).start()

    line = lax.broadcasted_iota(jnp.int32, (SUMS, rows), 0)
    local = lax.broadcasted_iota(jnp.int32, (SUMS, rows), 1)

    @pl.loop(0, count)
    def _(slot):
        col, row = grid_position((local + slot * rows).astype(jnp.float32))
        tags = jnp.where(line == 0, 1.0, jnp.where(line == 1, col, jnp.where(line == 2, row, 0.0)))
        places[slot] = tags.astype(jnp.bfloat16)

    top[...] = jnp.full_like(top, LOWEST)
    acc[...] = jnp.zeros_like(acc)
    load.wait()

    short = jnp.minimum(here, count - 1 - here)
    long_left = here > count - 1 - here

    def slot_of(item):
        paired = item <= 2 * short
        step = jnp.where(paired, (item + 1) // 2, item - short)
        left = jnp.where(paired, item % 2 == 1, long_left)
        return jnp.where(left, here - step, here + step)

    def arrive(slot, piece):
        pass_copy(slot, here, piece).wait_recv()

        @pl.when((slot < here) & has_right)
        def _():
            pass_copy(slot, here + 1, piece).start()

        @pl.when((slot > here) & has_left)
        def _():
            pass_copy(slot, here - 1, piece).start()

    def fold(slot):
        keys = held[slot]
        values = jnp.concatenate([keys.T, places[slot]], axis=0)
        for start in range(0, rows, WIDTH):
            some = slice(start, min(start + WIDTH, rows))
            scores = lax.dot_general(
                keys, queries[some], (((1,), (1,)), ((), ())), preferred_element_type=jnp.float32
            )
            old = top[:, some]
            new = jnp.maximum(old, jnp.max(scores, axis=0, keepdims=True))
            fade = jnp.exp2((old - new) * scale)
            weights = jnp.exp2((scores - new) * scale).astype(jnp.bfloat16)
            top[:, some] = new
            acc[:, some] = acc[:, some] * fade + jnp.dot(
                values, weights, preferred_element_type=jnp.float32
            )

    @pl.loop(0, count)
    def _(item):
        slot = slot_of(item)
        opens = (item % 2 == 1) & (item < 2 * short)
        second = (item > 0) & (item % 2 == 0) & (item <= 2 * short)
        for piece in range(PARTS):

            @pl.when(jnp.logical_not(second))
            def _():
                arrive(slot, piece)

            @pl.when(opens)
            def _():
                arrive(slot_of(item + 1), piece)

        fold(slot)

    inverse = 1.0 / acc[chans : chans + 1]
    matched[0, 0] = (acc[:chans] * inverse).T.astype(matched.dtype)
    means = acc[chans : chans + 8] * inverse
    index = (lax.broadcasted_iota(jnp.int32, (1, rows), 1) + here * rows).astype(jnp.float32)
    col, row = grid_position(index)
    flow[0, 0, 0:1] = (means[1:2] - col) * (1.0 / W)
    flow[0, 0, 1:2] = (means[2:3] - row) * (1.0 / W)

    for piece in range(PARTS):
        own_copy(0, here, piece).wait_send()

        @pl.when(has_left)
        def _():
            own_copy(1, here - 1, piece).wait_send()

        @pl.when(has_right)
        def _():
            own_copy(2, here + 1, piece).wait_send()

    @pl.loop(0, count)
    def _(slot):
        sent = ((slot < here) & has_right) | ((slot > here) & has_left)

        @pl.when(sent)
        def _():
            for piece in range(PARTS):
                pass_copy(slot, here, piece).wait_send()


def write_out(flow_in, matched_in, flow, matched, flow_sem, matched_sem):
    flow_copy = pltpu.make_async_copy(flow_in, flow, flow_sem)
    matched_copy = pltpu.make_async_copy(matched_in, matched, matched_sem)
    matched_copy.start()
    flow_copy.start()
    matched_copy.wait()
    flow_copy.wait()


def body(count, features):
    rows, chans = features.shape[2], features.shape[3]
    shapes = (
        jax.ShapeDtypeStruct((1, 1, 2, rows), jnp.float32),
        jax.ShapeDtypeStruct((1, 1, rows, chans), jnp.bfloat16),
    )
    flow, matched = pl.pallas_call(
        functools.partial(kernel, count),
        out_shape=shapes,
        in_specs=[pl.BlockSpec(memory_space=pl.ANY)],
        out_specs=(
            pl.BlockSpec(memory_space=pltpu.VMEM),
            pl.BlockSpec(memory_space=pltpu.VMEM),
        ),
        scratch_shapes=[
            pltpu.VMEM((rows, chans), jnp.bfloat16),
            pltpu.VMEM((count, rows, chans), jnp.bfloat16),
            pltpu.VMEM((count, SUMS, rows), jnp.bfloat16),
            pltpu.VMEM((1, rows), jnp.float32),
            pltpu.VMEM((chans + SUMS, rows), jnp.float32),
            pltpu.SemaphoreType.DMA((3, PARTS)),
            pltpu.SemaphoreType.DMA((count, PARTS)),
            pltpu.SemaphoreType.DMA((count, PARTS)),
            pltpu.SemaphoreType.DMA,
        ],
        compiler_params=pltpu.CompilerParams(
            collective_id=0, has_side_effects=True, vmem_limit_bytes=LIMIT
        ),
    )(features)
    return pl.pallas_call(
        write_out,
        out_shape=shapes,
        in_specs=[pl.BlockSpec(memory_space=pl.ANY)] * 2,
        out_specs=[pl.BlockSpec(memory_space=pl.ANY)] * 2,
        scratch_shapes=[pltpu.SemaphoreType.DMA, pltpu.SemaphoreType.DMA],
        compiler_params=pltpu.CompilerParams(vmem_limit_bytes=2**20),
    )(flow, matched)


def solution(mesh):
    placed = (P(("clips", "pair"), "dir", "pix", None),)
    return jax.shard_map(
        functools.partial(body, mesh.shape["pix"]),
        mesh=mesh,
        in_specs=placed,
        out_specs=(
            P(("clips", "pair"), "dir", None, "pix"),
            P(("clips", "pair"), "dir", "pix", None),
        ),
        check_vma=False,
    )
```

time: 27.3 us -> 18.3 us (0.67)
  blocking collectives: 17.3 us -> 0 us
  Pallas kernels: 0 us -> 16.6 us
  other arithmetic: 2.18 us -> 0 us
  matrix products: 2.06 us -> 0 us
  loops' own time: 1.38 us -> 0 us
  starting transfers between devices: 1.15 us -> 0 us
  local copies, waits for them, and re-layouts: 1.84 us -> 0.89 us
  waiting for transfers between devices: 0.44 us -> 0 us
    all_gather x1 -> x0, blocking collectives: 17.3 us -> none  [body(): lax.all_gather(features, 'pix', axis=2, tiled=True)]
    pallas_call x0 -> x2, Pallas kernels: none -> 16.6 us  [the longest x1 16 us: body(): pl.pallas_call(functools.partial(kernel, count), out_shape=shapes, in_spe...]
    dot_general x4 -> x0, matrix products: 2.06 us -> none  [the longest x2 1.06 us: fold_part(): jnp.dot(weights.astype(jnp.bfloat16), keys, preferred_element_type=jnp.fl...]
    another operation x1 -> x0, loops' own time: 1.38 us -> none  [make_step(): lax.scan(inner, carry, (blocks, jnp.arange(length // width, dtype=jnp.int...]
    reduce_sum x2 -> x0, other arithmetic: 1.29 us -> none  [fold_part(): sum_y = sum_y * fade + jnp.sum(weights * posy[None, :], axis=1)]
    dynamic_slice x2 -> x0, local copies, waits for them, and re-layouts: 1.17 us -> none  [make_step(): lax.scan(inner, carry, (blocks, jnp.arange(length // width, dtype=jnp.int...]
    ppermute x3 -> x0, starting transfers between devices: 1.15 us -> none  [from_partner(): lax.ppermute(array, axis, [(i, i ^ 1 << bit) for i in range(lax.axis_size...]
    reshape x1 -> x0, other arithmetic: 0.6 us -> none  [body(): flow.reshape(1, 1, 2, rows_here)]
  transfers between devices with their start and end apart: 3 -> 0, of which waited for: 1 -> 0; matrix products, arithmetic and copies ran while one was open for 3% -> 0% of each run, Pallas kernels for 0% -> 0%
where the time goes in v1:
time: 18.3 us; the launch traced here: 18.2 us
  Pallas kernels  16.6 us (91%)
  local copies, waits for them, and re-layouts  0.89 us (5%)
  between operations  0.65 us (4%)
    pallas_call x1, Pallas kernels, body(): pl.pallas_call(functools.partial(kernel, count), out_shape=shapes, in_spe...  16 us
    unnamed x2, local copies, waits for them, and re-layouts  0.89 us
    pallas_call x1, Pallas kernels, body(): pl.pallas_call(write_out, out_shape=shapes, in_specs=[pl.BlockSpec(memory...  0.67 us

profile of v1, /device:TPU:0, one launch (start us, length us, event | category | flops | bytes accessed | tf_op | source)
XLA Modules:
  0.0 18.2 jit_solution(13206572060647134013)
XLA Ops:
  0.6 0.0 copy-start
  0.6 0.9 %copy-done = bf16[1,1,480,128]{3,2,1,0:T(8,128)(2,1)S(1)} copy-done((bf16[1,1,480,128]{3,2,1,0:T(8,128)(2,1)S(1)}, bf16[1,1,480,128]{3,2,1,0:T(8,128)(2,1)}, u32[]{:S(2)}) %copy-start) | copy-done | bytes 122904
  1.5 16.0 %shard_map.30 = (f32[1,1,2,480]{3,2,1,0:T(2,128)S(1)}, bf16[1,1,480,128]{3,2,1,0:T(8,128)(2,1)S(1)}) custom-call(bf16[1,1,480,128]{3,2,1,0:T(8,128)(2,1)S(1)} %copy-done), custom_call_target="tpu_custom_call" | custom-call | tf_op jit(solution)/shard_map/pallas_call | solution.py:208
  17.5 0.7 %shard_map.31 = (f32[1,1,2,480]{3,2,1,0:T(2,128)}, bf16[1,1,480,128]{3,2,1,0:T(8,128)(2,1)}) custom-call(f32[1,1,2,480]{3,2,1,0:T(2,128)S(1)} %get-tuple-element.4.flow_in, bf16[1,1,480,128]{3,2,1,0:T(8,128)(2,1)S(1)} %get-tuple-element.5.matched_in), custom_call_target="tpu_custom_call" | custom-call | tf_op jit(solution)/shard_map/pallas_call | solution.py:231
Async XLA Ops:
  0.6 0.9 %copy-start = (bf16[1,1,480,128]{3,2,1,0:T(8,128)(2,1)S(1)}, bf16[1,1,480,128]{3,2,1,0:T(8,128)(2,1)}, u32[]{:S(2)}) copy-start(bf16[1,1,480,128]{3,2,1,0:T(8,128)(2,1)} %feats.1) | copy-start | bytes 368644

commit v2 on v1

--- a/solution.py
+++ b/solution.py
@@ -127,9 +127,9 @@
         def _():
             pass_copy(slot, here - 1, piece).start()
 
-    def fold(slot):
-        keys = held[slot]
-        values = jnp.concatenate([keys.T, places[slot]], axis=0)
+    def fold(slot, first, length):
+        keys = held[slot, first : first + length]
+        values = jnp.concatenate([keys.T, places[slot, :, first : first + length]], axis=0)
         for start in range(0, rows, WIDTH):
             some = slice(start, min(start + WIDTH, rows))
             scores = lax.dot_general(
@@ -144,7 +144,7 @@
                 values, weights, preferred_element_type=jnp.float32
             )
 
-    @pl.loop(0, count)
+    @pl.loop(0, count - 1)
     def _(item):
         slot = slot_of(item)
         opens = (item % 2 == 1) & (item < 2 * short)
@@ -159,7 +159,16 @@
             def _():
                 arrive(slot_of(item + 1), piece)
 
-        fold(slot)
+        fold(slot, 0, rows)
+
+    final = slot_of(count - 1)
+    for piece in range(PARTS):
+
+        @pl.when((here == 0) | (here == count - 1) | (count > 2 * short + 1))
+        def _():
+            arrive(final, piece)
+
+        fold(final, piece * part, part)
 
     inverse = 1.0 / acc[chans : chans + 1]
     matched[0, 0] = (acc[:chans] * inverse).T.astype(matched.dtype)

time: 18.3 us -> 18.2 us (level)
  no operation moved by 1% of the time
where the time goes in v2:
time: 18.2 us; the launch traced here: 18 us
  Pallas kernels  16.5 us (91%)
  local copies, waits for them, and re-layouts  0.89 us (5%)
  between operations  0.65 us (4%)
    pallas_call x1, Pallas kernels, body(): pl.pallas_call(functools.partial(kernel, count), out_shape=shapes, in_spe...  15.8 us
    unnamed x2, local copies, waits for them, and re-layouts  0.89 us
    pallas_call x1, Pallas kernels, body(): pl.pallas_call(write_out, out_shape=shapes, in_specs=[pl.BlockSpec(memory...  0.67 us

profile of v2, /device:TPU:0, one launch (start us, length us, event | category | flops | bytes accessed | tf_op | source)
XLA Modules:
  0.0 18.0 jit_solution(17549503832912086936)
XLA Ops:
  0.6 0.0 copy-start
  0.6 0.9 %copy-done = bf16[1,1,480,128]{3,2,1,0:T(8,128)(2,1)S(1)} copy-done((bf16[1,1,480,128]{3,2,1,0:T(8,128)(2,1)S(1)}, bf16[1,1,480,128]{3,2,1,0:T(8,128)(2,1)}, u32[]{:S(2)}) %copy-start) | copy-done | bytes 122904
  1.5 15.8 %shard_map.30 = (f32[1,1,2,480]{3,2,1,0:T(2,128)S(1)}, bf16[1,1,480,128]{3,2,1,0:T(8,128)(2,1)S(1)}) custom-call(bf16[1,1,480,128]{3,2,1,0:T(8,128)(2,1)S(1)} %copy-done), custom_call_target="tpu_custom_call" | custom-call | tf_op jit(solution)/shard_map/pallas_call | solution.py:217
  17.4 0.7 %shard_map.31 = (f32[1,1,2,480]{3,2,1,0:T(2,128)}, bf16[1,1,480,128]{3,2,1,0:T(8,128)(2,1)}) custom-call(f32[1,1,2,480]{3,2,1,0:T(2,128)S(1)} %get-tuple-element.4.flow_in, bf16[1,1,480,128]{3,2,1,0:T(8,128)(2,1)S(1)} %get-tuple-element.5.matched_in), custom_call_target="tpu_custom_call" | custom-call | tf_op jit(solution)/shard_map/pallas_call | solution.py:240
Async XLA Ops:
  0.6 0.9 %copy-start = (bf16[1,1,480,128]{3,2,1,0:T(8,128)(2,1)S(1)}, bf16[1,1,480,128]{3,2,1,0:T(8,128)(2,1)}, u32[]{:S(2)}) copy-start(bf16[1,1,480,128]{3,2,1,0:T(8,128)(2,1)} %feats.1) | copy-start | bytes 368644

commit v3 on v2

--- a/solution.py
+++ b/solution.py
@@ -13,7 +13,7 @@
 PARTS = 2
 WIDTH = 512
 SUMS = 16
-LIMIT = 40 * 2**20
+LIMIT = 55056 * 2**10
 MESH = pl.DeviceIdType.MESH
 
 

time: 18.2 us -> 17.4 us (0.956)
  local copies, waits for them, and re-layouts: 0.89 us -> 0 us
    unnamed x2 -> x0, local copies, waits for them, and re-layouts: 0.89 us -> none
where the time goes in v3:
time: 17.4 us; the launch traced here: 17.3 us
  Pallas kernels  16.6 us (95%)
  between operations  0.64 us (4%)
    pallas_call x1, Pallas kernels, body(): pl.pallas_call(functools.partial(kernel, count), out_shape=shapes, in_spe...  16 us
    pallas_call x1, Pallas kernels, body(): pl.pallas_call(write_out, out_shape=shapes, in_specs=[pl.BlockSpec(memory...  0.67 us

profile of v3, /device:TPU:0, one launch (start us, length us, event | category | flops | bytes accessed | tf_op | source)
XLA Modules:
  0.0 17.3 jit_solution(16042206382332134685)
XLA Ops:
  0.6 16.0 %shard_map.30 = (f32[1,1,2,480]{3,2,1,0:T(2,128)S(1)}, bf16[1,1,480,128]{3,2,1,0:T(8,128)(2,1)S(1)}) custom-call(bf16[1,1,480,128]{3,2,1,0:T(8,128)(2,1)} %feats.1), custom_call_target="tpu_custom_call" | custom-call | tf_op jit(solution)/shard_map/pallas_call | solution.py:217
  16.6 0.7 %shard_map.31 = (f32[1,1,2,480]{3,2,1,0:T(2,128)}, bf16[1,1,480,128]{3,2,1,0:T(8,128)(2,1)}) custom-call(f32[1,1,2,480]{3,2,1,0:T(2,128)S(1)} %get-tuple-element.4.flow_in, bf16[1,1,480,128]{3,2,1,0:T(8,128)(2,1)S(1)} %get-tuple-element.5.matched_in), custom_call_target="tpu_custom_call" | custom-call | tf_op jit(solution)/shard_map/pallas_call | solution.py:240

commit v4 on v3

--- a/solution.py
+++ b/solution.py
@@ -10,7 +10,7 @@
 
 W = 120
 LOWEST = -1e30
-PARTS = 2
+PARTS = 3
 WIDTH = 512
 SUMS = 16
 LIMIT = 55056 * 2**10
@@ -23,7 +23,7 @@
 
 
 def kernel(
-    count, feats, flow, matched, queries, held, places, top, acc, own_sem, pass_sem, recv_sem, load_sem
+    count, feats, flow, matched, queries, held, places, top, acc, own_sem, pass_sem, recv_sem, load_sem, ready
 ):
     rows, chans = feats.shape[2], feats.shape[3]
     part = rows // PARTS
@@ -39,25 +39,19 @@
 
     barrier = pltpu.get_barrier_semaphore()
 
-    def greet(pix, core):
+    def greet(sem, pix, core):
         pl.semaphore_signal(
-            barrier, inc=1, device_id={"pix": pix, "dir": core}, device_id_type=MESH
+            sem, inc=1, device_id={"pix": pix, "dir": core}, device_id_type=MESH
         )
 
-    greet(here, other)
-
-    @pl.when(has_left)
-    def _():
-        greet(here - 1, other)
-        greet(here - 1, side)
+    greet(barrier, here, other)
 
     @pl.when(has_right)
     def _():
-        greet(here + 1, other)
-        greet(here + 1, side)
-
-    neighbours = has_left.astype(jnp.int32) + has_right.astype(jnp.int32)
-    pl.semaphore_wait(barrier, 1 + 2 * neighbours)
+        greet(barrier, here + 1, other)
+        greet(barrier, here + 1, side)
+
+    pl.semaphore_wait(barrier, 1 + 2 * has_left.astype(jnp.int32))
 
     def own_copy(which, pix, piece):
         span = pl.ds(piece * part, part)
@@ -81,18 +75,21 @@
             device_id_type=MESH,
         )
 
-    for piece in range(PARTS):
-
-        @pl.when(has_left)
-        def _():
+    @pl.when(has_left)
+    def _():
+        greet(ready, here - 1, other)
+        greet(ready, here - 1, side)
+        for piece in range(PARTS):
             own_copy(1, here - 1, piece).start()
-
-        @pl.when(has_right)
-        def _():
-            own_copy(2, here + 1, piece).start()
 
     for piece in range(PARTS):
         own_copy(0, here, piece).start()
+
+    @pl.when(has_right)
+    def _():
+        pl.semaphore_wait(ready, 2)
+        for piece in range(PARTS):
+            own_copy(2, here + 1, piece).start()
 
     line = lax.broadcasted_iota(jnp.int32, (SUMS, rows), 0)
     local = lax.broadcasted_iota(jnp.int32, (SUMS, rows), 1)
@@ -232,6 +229,7 @@
             pltpu.SemaphoreType.DMA((count, PARTS)),
             pltpu.SemaphoreType.DMA((count, PARTS)),
             pltpu.SemaphoreType.DMA,
+            pltpu.SemaphoreType.REGULAR,
         ],
         compiler_params=pltpu.CompilerParams(
             collective_id=0, has_side_effects=True, vmem_limit_bytes=LIMIT

time: 17.4 us -> 17.3 us (level)
  no operation moved by 1% of the time
where the time goes in v4:
time: 17.3 us; the launch traced here: 17.2 us
  Pallas kernels  16.5 us (95%)
  between operations  0.64 us (4%)
    pallas_call x1, Pallas kernels, body(): pl.pallas_call(functools.partial(kernel, count), out_shape=shapes, in_spe...  15.8 us
    pallas_call x1, Pallas kernels, body(): pl.pallas_call(write_out, out_shape=shapes, in_specs=[pl.BlockSpec(memory...  0.67 us

profile of v4, /device:TPU:0, one launch (start us, length us, event | category | flops | bytes accessed | tf_op | source)
XLA Modules:
  0.0 17.2 jit_solution(16929940200650557279)
XLA Ops:
  0.6 15.8 %shard_map.30 = (f32[1,1,2,480]{3,2,1,0:T(2,128)S(1)}, bf16[1,1,480,128]{3,2,1,0:T(8,128)(2,1)S(1)}) custom-call(bf16[1,1,480,128]{3,2,1,0:T(8,128)(2,1)} %feats.1), custom_call_target="tpu_custom_call" | custom-call | tf_op jit(solution)/shard_map/pallas_call | solution.py:214
  16.5 0.7 %shard_map.31 = (f32[1,1,2,480]{3,2,1,0:T(2,128)}, bf16[1,1,480,128]{3,2,1,0:T(8,128)(2,1)}) custom-call(f32[1,1,2,480]{3,2,1,0:T(2,128)S(1)} %get-tuple-element.4.flow_in, bf16[1,1,480,128]{3,2,1,0:T(8,128)(2,1)S(1)} %get-tuple-element.5.matched_in), custom_call_target="tpu_custom_call" | custom-call | tf_op jit(solution)/shard_map/pallas_call | solution.py:238

commit v5 on v3

--- a/solution.py
+++ b/solution.py
@@ -10,7 +10,7 @@
 
 W = 120
 LOWEST = -1e30
-PARTS = 2
+PARTS = 3
 WIDTH = 512
 SUMS = 16
 LIMIT = 55056 * 2**10

time: 17.4 us -> 17.2 us (0.989)
  Pallas kernels: 16.6 us -> 16.4 us
    pallas_call x1, Pallas kernels: 16 us -> 15.7 us  [body(): pl.pallas_call(functools.partial(kernel, count), out_shape=shapes, in_spe...]
where the time goes in v5:
time: 17.2 us; the launch traced here: 17.1 us
  Pallas kernels  16.4 us (95%)
  between operations  0.64 us (4%)
    pallas_call x1, Pallas kernels, body(): pl.pallas_call(functools.partial(kernel, count), out_shape=shapes, in_spe...  15.7 us
    pallas_call x1, Pallas kernels, body(): pl.pallas_call(write_out, out_shape=shapes, in_specs=[pl.BlockSpec(memory...  0.67 us

profile of v5, /device:TPU:0, one launch (start us, length us, event | category | flops | bytes accessed | tf_op | source)
XLA Modules:
  0.0 17.1 jit_solution(10683984346903583882)
XLA Ops:
  0.6 15.7 %shard_map.30 = (f32[1,1,2,480]{3,2,1,0:T(2,128)S(1)}, bf16[1,1,480,128]{3,2,1,0:T(8,128)(2,1)S(1)}) custom-call(bf16[1,1,480,128]{3,2,1,0:T(8,128)(2,1)} %feats.1), custom_call_target="tpu_custom_call" | custom-call | tf_op jit(solution)/shard_map/pallas_call | solution.py:217
  16.4 0.7 %shard_map.31 = (f32[1,1,2,480]{3,2,1,0:T(2,128)}, bf16[1,1,480,128]{3,2,1,0:T(8,128)(2,1)}) custom-call(f32[1,1,2,480]{3,2,1,0:T(2,128)S(1)} %get-tuple-element.4.flow_in, bf16[1,1,480,128]{3,2,1,0:T(8,128)(2,1)S(1)} %get-tuple-element.5.matched_in), custom_call_target="tpu_custom_call" | custom-call | tf_op jit(solution)/shard_map/pallas_call | solution.py:240

commit v6 on v5

--- a/solution.py
+++ b/solution.py
@@ -86,6 +86,8 @@
         @pl.when(has_left)
         def _():
             own_copy(1, here - 1, piece).start()
+
+    for piece in range(PARTS):
 
         @pl.when(has_right)
         def _():
@@ -171,7 +173,7 @@
         fold(final, piece * part, part)
 
     inverse = 1.0 / acc[chans : chans + 1]
-    matched[0, 0] = (acc[:chans] * inverse).T.astype(matched.dtype)
+    matched[0, 0] = (acc[:chans] * inverse).astype(matched.dtype).T
     means = acc[chans : chans + 8] * inverse
     index = (lax.broadcasted_iota(jnp.int32, (1, rows), 1) + here * rows).astype(jnp.float32)
     col, row = grid_position(index)

time: 17.2 us -> 17.2 us (level)
  no operation moved by 1% of the time
where the time goes in v6:
time: 17.2 us; the launch traced here: 17 us
  Pallas kernels  16.4 us (95%)
  between operations  0.64 us (4%)
    pallas_call x1, Pallas kernels, body(): pl.pallas_call(functools.partial(kernel, count), out_shape=shapes, in_spe...  15.7 us
    pallas_call x1, Pallas kernels, body(): pl.pallas_call(write_out, out_shape=shapes, in_specs=[pl.BlockSpec(memory...  0.67 us

profile of v6, /device:TPU:0, one launch (start us, length us, event | category | flops | bytes accessed | tf_op | source)
XLA Modules:
  0.0 17.0 jit_solution(4499565588249065274)
XLA Ops:
  0.6 15.7 %shard_map.30 = (f32[1,1,2,480]{3,2,1,0:T(2,128)S(1)}, bf16[1,1,480,128]{3,2,1,0:T(8,128)(2,1)S(1)}) custom-call(bf16[1,1,480,128]{3,2,1,0:T(8,128)(2,1)} %feats.1), custom_call_target="tpu_custom_call" | custom-call | tf_op jit(solution)/shard_map/pallas_call | solution.py:219
  16.4 0.7 %shard_map.31 = (f32[1,1,2,480]{3,2,1,0:T(2,128)}, bf16[1,1,480,128]{3,2,1,0:T(8,128)(2,1)}) custom-call(f32[1,1,2,480]{3,2,1,0:T(2,128)S(1)} %get-tuple-element.4.flow_in, bf16[1,1,480,128]{3,2,1,0:T(8,128)(2,1)S(1)} %get-tuple-element.5.matched_in), custom_call_target="tpu_custom_call" | custom-call | tf_op jit(solution)/shard_map/pallas_call | solution.py:242
